TPU v7x, 512 devices: a whole 4x4x16 slice. The times are simulated.
512 devices in a mesh: seq: 128 (over z, y, core), head: 4 (over x).
Axes of the slice: x: 4, y: 4, z: 16, core: 2. Of those that a mesh axis runs over, the one named last changes fastest.
Arguments:
- patches: bfloat16 [32768, 1280], P('seq'), may hold values from -6 to 6
- norm_gain: float32 [1280], replicated, may hold values from 0.5 to 1.5
- w_qkv: bfloat16 [1280, 3, 1280], P('seq', None, 'head'), as said below
- w_out: bfloat16 [1280, 1280], P('head', 'seq'), may hold values from -0.15625 to 0.15625
- window_order: int32 [128, 64], P('seq'), may hold values from 0 to 63, each once within a row
- merge_gain: float32 [1280], replicated, may hold values from 0.5 to 1.5
- w_kv: bfloat16 [5120, 2, 1024], P('seq', None, 'head'), as said below
- queries: bfloat16 [256, 8192], P('seq', 'head'), may hold values from -6 to 6
- suffix_kv: bfloat16 [256, 64, 2, 1024], P('seq', None, None, 'head'), may hold values from -12 to 12
- question_lengths: int32 [256], P('seq'), may hold values from 1 to 64
- frame_range: int32 [256, 2], replicated, may hold values from 0 to 128, as said below
Outputs:
- answers: bfloat16 [256, 8192], P('seq', 'head')
Inputs may be any that keep to these rules, and one draw needn't show every extreme that they name: `window_order`: each row is an ordering of a frame's units; positions w * 16 to (w + 1) * 16 - 1 form window w. `frame_range`: the first entry of a row is below the second. `w_qkv`: entries of order one over the square root of 1280. `w_kv`: entries of order one over the square root of 5120.
All inputs are finite; a program needn't handle non-finite values.
Results may differ from a plain program's by a relative error of at most 0.007.
Values may be sent and summed in bfloat16 or wider, within the bound.
No kernel may reach another device: no remote copies, remote signals or barrier semaphores. Data moves between devices by JAX's collectives and lax.ppermute only.
A program may use at most 64 MiB of HBM per device.

v0:
```python
import jax
import jax.numpy as jnp
from jax import lax
from jax.sharding import Mesh
from jax.sharding import PartitionSpec as P

VD = 1280
VH = 16
HD = 128
FPATCH = 256
WIN = 64
SEQ = ("seq_0", "seq_1", "seq_2")
NEGATIVE = -1e30


def in_order(blocks, dim):
    dims = list(blocks.shape[1:])
    dims[dim] *= blocks.shape[0]
    return jnp.moveaxis(blocks, 0, dim).reshape(dims)


def all_blocks(value, axes, sequence):
    blocks = value[None]
    for k in sequence:
        blocks = lax.all_gather(blocks, axes[k], axis=0, tiled=True)
    current = [lax.axis_size(axes[k]) for k in reversed(sequence)]
    blocks = blocks.reshape(*current, *value.shape)
    turned = sorted(range(len(sequence)), key=lambda place: sequence[len(sequence) - 1 - place])
    return blocks.transpose(*turned, *range(len(sequence), blocks.ndim)).reshape(-1, *value.shape)


def whole_of(value, axes, sequence, dim):
    return in_order(all_blocks(value, axes, sequence), dim)


def from_everyone(value, axis):
    copies = jnp.broadcast_to(value, (lax.axis_size(axis), *value.shape))
    return lax.all_to_all(copies, axis, split_axis=0, concat_axis=0, tiled=True)


def of_everyone(value, axis):
    everything = from_everyone(value, axis)
    return jnp.sum(everything.astype(jnp.float32), axis=0)


def rms_scale(values, gain):
    return values * lax.rsqrt(jnp.mean(values * values, axis=-1, keepdims=True) + 1e-06) * gain


def frame_window(frame_rows, unit_order, local_heads, head_size):
    unit_count = unit_order.shape[0]
    grouped = frame_rows.reshape(unit_count, 4, 3, local_heads * head_size)[unit_order]
    windows = grouped.reshape(-1, WIN, 3, local_heads, head_size)
    scores = jnp.einsum(
        "wqhd,wkhd->whqk", windows[:, :, 0], windows[:, :, 1], preferred_element_type=jnp.float32
    ) * head_size ** (-0.5)
    weights = jax.nn.softmax(scores, axis=-1).astype(jnp.bfloat16)
    mixed = jnp.einsum(
        "whqk,wkhd->wqhd", weights, windows[:, :, 2], preferred_element_type=jnp.float32
    ).astype(jnp.bfloat16)
    mixed = mixed.reshape(unit_count, 4, local_heads * head_size)
    return (
        jnp.zeros_like(mixed)
        .at[unit_order]
        .set(mixed)
        .reshape(unit_count * 4, local_heads * head_size)
    )


def prefix_scores(asking, keys_values, bounds, frame_tokens):
    token_count = keys_values.shape[0]
    kv_local, head_size = (asking.shape[1], asking.shape[3])
    keys = keys_values[:, 0].reshape(token_count, kv_local, head_size)
    values = keys_values[:, 1].reshape(token_count, kv_local, head_size)
    frame_index = jnp.arange(token_count) // frame_tokens
    live = (frame_index[None, :] >= bounds[:, 0:1]) & (frame_index[None, :] < bounds[:, 1:2])
    scores = jnp.einsum(
        "qgjd,ngd->qgjn", asking, keys, preferred_element_type=jnp.float32
    ) * head_size ** (-0.5)
    return (jnp.where(live[:, None, None, :], scores, -jnp.inf), values)


def add_suffix(maxima, totals, weighted, asking, suffix_kv, lengths):
    quest_count, span = (suffix_kv.shape[0], suffix_kv.shape[1])
    kv_local, head_size = (asking.shape[1], asking.shape[3])
    keys = suffix_kv[:, :, 0].reshape(quest_count, span, kv_local, head_size)
    values = suffix_kv[:, :, 1].reshape(quest_count, span, kv_local, head_size)
    scores = jnp.einsum(
        "qgjd,qsgd->qgjs", asking, keys, preferred_element_type=jnp.float32
    ) * head_size ** (-0.5)
    live = (jnp.arange(span)[None, :] < lengths[:, None])[:, None, None, :]
    scores = jnp.where(live, scores, -jnp.inf)
    highest = jnp.maximum(maxima, jnp.max(scores, axis=-1))
    weights = jnp.exp(scores - highest[..., None])
    carried = jnp.exp(maxima - highest)
    totals = totals * carried + jnp.sum(weights, axis=-1)
    weighted = weighted * carried[..., None] + jnp.einsum(
        "qgjs,qsgd->qgjd", weights.astype(jnp.bfloat16), values, preferred_element_type=jnp.float32
    )
    return (weighted / totals[..., None]).reshape(quest_count, -1).astype(jnp.bfloat16)


def on_device(
    patches,
    norm_gain,
    w_qkv,
    w_out,
    window_order,
    merge_gain,
    w_kv,
    queries,
    suffix_kv,
    question_lengths,
    frame_range,
):
    row_count = patches.shape[0]
    columns = w_qkv.shape[2]
    head_size = VD // VH
    local_heads = columns // head_size
    source = patches.astype(jnp.float32)
    normed = rms_scale(source, norm_gain).astype(jnp.bfloat16)
    portion = whole_of(w_qkv, SEQ, (1, 0, 2), 0)
    inputs = normed
    projected = jnp.dot(
        inputs, portion.reshape(portion.shape[0], 3 * columns), preferred_element_type=jnp.float32
    )
    projected = projected.astype(jnp.bfloat16).reshape(window_order.shape[0], -1, 3, columns)
    attended = jax.vmap(
        lambda frame_rows, unit_order: frame_window(frame_rows, unit_order, local_heads, head_size)
    )(projected, window_order)
    attended = attended.reshape(row_count, columns)
    w_full = lax.all_gather(w_out, SEQ, axis=1, tiled=True)
    summed = of_everyone(
        jnp.dot(attended, w_full, preferred_element_type=jnp.float32).astype(jnp.bfloat16), "head"
    ).astype(jnp.float32)
    merged_all = (
        rms_scale(source + summed, merge_gain).astype(jnp.bfloat16).reshape(row_count // 4, 4 * VD)
    )
    token_count = merged_all.shape[0]
    kv_columns = w_kv.shape[2]
    portion = lax.all_gather(w_kv, SEQ, axis=0, tiled=True)
    inputs = merged_all
    visual = jnp.dot(
        inputs,
        portion.reshape(portion.shape[0], 2 * kv_columns),
        preferred_element_type=jnp.float32,
    )
    visual = visual.astype(jnp.bfloat16).reshape(token_count, 2, kv_columns)
    quest_count = queries.shape[0]
    kv_local = kv_columns // HD
    asking = queries.reshape(quest_count, kv_local, -1, HD)
    group = asking.shape[2]
    frame_tokens = FPATCH // 4
    seq_index = lax.axis_index(SEQ)
    own_bounds = lax.dynamic_slice_in_dim(frame_range, seq_index * quest_count, quest_count, 0)
    maxima = jnp.full((quest_count, kv_local, group), NEGATIVE, jnp.float32)
    scores, values = prefix_scores(
        asking, whole_of(visual, SEQ, (1, 0, 2), 0), own_bounds, frame_tokens
    )
    highest = jnp.maximum(maxima, jnp.max(scores, axis=-1))
    weights = jnp.exp(scores - highest[..., None])
    totals = jnp.sum(weights, axis=-1)
    weighted = jnp.einsum(
        "qgjn,ngd->qgjd", weights.astype(jnp.bfloat16), values, preferred_element_type=jnp.float32
    )
    maxima, totals, weighted = (highest, totals, weighted)
    return add_suffix(maxima, totals, weighted, asking, suffix_kv, question_lengths)


def solution(mesh):
    torus = Mesh(
        mesh.devices.reshape(16, 4, 2, mesh.shape["head"]), ("seq_0", "seq_1", "seq_2", "head")
    )
    in_specs = (
        P(SEQ, None),
        P(),
        P(SEQ, None, "head"),
        P("head", SEQ),
        P(SEQ, None),
        P(),
        P(SEQ, None, "head"),
        P(SEQ, "head"),
        P(SEQ, None, None, "head"),
        P(SEQ),
        P(),
    )
    out_specs = P(SEQ, "head")
    return jax.shard_map(
        on_device, mesh=torus, in_specs=in_specs, out_specs=out_specs, check_vma=False
    )
```

profile of v0, /device:TPU:1, one launch (start us, length us, event | category | flops | bytes accessed | tf_op | source)
XLA Modules:
  0.0 429.4 jit_solution(2125874026757927389)
XLA Ops:
  6.5 12.5 %all-gather = bf16[40,3,320]{2,1,0:T(4,128)(2,1)} all-gather(bf16[10,3,320]{2,1,0:T(4,128)(2,1)} %param.13), channel_id=2, replica_groups=mesh['seq_0'=16,'seq_1'=4,'seq_2'=2,'head'=4] {'seq_1'}, dimensions={0}, use_global_device_ids=true | all-gather | bytes 96000 | tf_op jit(solution)/shard_map/all_gather | solution.py:25
  19.1 69.1 %all-gather.8.cloned.1.call-done = bf16[64,10,3,320]{3,2,1,0:T(4,128)(2,1)} async-done(((bf16[4,10,3,320]{3,2,1,0:T(4,128)(2,1)}), bf16[64,10,3,320]{3,2,1,0:T(4,128)(2,1)}) %all-gather.8.cloned.1.call-update) | async-done | bytes 1228816 | tf_op jit(solution)/shard_map/all_gather | solution.py:25
  88.2 3.1 copy.104
  92.1 111.3 %all-gather.1 = bf16[128,10,320]{2,1,0:T(8,128)(2,1)S(1)} all-gather(bf16[1,10,320]{2,1,0:T(8,128)(2,1)S(1)} %bitcast.119), channel_id=1, replica_groups=mesh['seq_0'=16,'seq_1'=4,'seq_2'=2,'head'=4] {'seq_0','seq_1','seq_2'}, dimensions={0}, use_global_device_ids=true | all-gather | bytes 825600 | tf_op jit(solution)/shard_map/all_gather | solution.py:132
  203.4 1.5 reshape.215
  205.2 4.6 %reshape.179 = bf16[2,16,4,10,3,320]{5,2,1,0,4,3:T(4,128)(2,1)S(1)} reshape(bf16[128,10,3,320]{3,0,2,1:T(8,128)(2,1)} %all-gather.10.cloned.1.call-done) | data formatting | bytes 4915200 | tf_op jit(solution)/shard_map/reshape | solution.py:27
  209.8 4.5 %copy.105 = bf16[16,4,2,10,3,320]{5,4,3,2,1,0:T(4,128)(2,1)} copy(bf16[16,4,2,10,3,320]{5,1,0,2,4,3:T(4,128)(2,1)S(1)} %bitcast.112) | data formatting | bytes 4915200 | tf_op jit(solution)/shard_map/transpose | solution.py:29
  214.3 7.0 %reshape_reshape_reshape.3 = bf16[1280,960]{1,0:T(8,128)(2,1)S(1)} reshape(bf16[16,4,2,10,3,320]{5,4,3,2,1,0:T(4,128)(2,1)} %copy.105) | data formatting | bytes 4915200 | tf_op jit(solution)/shard_map/reshape;reshape;reshape | solution.py:125
  221.3 2.0 convolution_convert_fusion.1
  223.3 1.2 copy.106
  225.2 1.1 gather_fusion
  228.9 2.5 scatter_fusion
  232.2 35.4 %all_to_all.5 = bf16[4,256,1280]{2,1,0:T(8,128)(2,1)S(1)} all-to-all(bf16[4,256,1280]{2,1,0:T(8,128)(2,1)S(1)} %broadcast_in_dim.37), channel_id=1, replica_groups=mesh['seq_0'=16,'seq_1'=4,'seq_2'=2,'head'=4] {'head'}, dimensions={0} | all-to-all | bytes 5242880 | tf_op jit(solution)/shard_map/all_to_all | solution.py:38
  269.0 3.4 copy.144
  272.4 1.0 convolution_convert_fusion.3
  273.5 11.1 %all_gather.29 = bf16[4,64,2,256]{3,1,2,0:T(8,128)(2,1)} all-gather(bf16[1,64,2,256]{3,1,2,0:T(8,128)(2,1)S(1)} %copy.114), channel_id=1, replica_groups=mesh['seq_0'=16,'seq_1'=4,'seq_2'=2,'head'=4] {'seq_1'}, dimensions={0}, use_global_device_ids=true | all-gather | bytes 327680 | tf_op jit(solution)/shard_map/all_gather | solution.py:25
  284.7 66.7 %all-gather.14.cloned.1.call-done = bf16[64,64,2,256]{3,1,2,0:T(8,128)(2,1)} async-done(((bf16[4,64,2,256]{3,1,2,0:T(8,128)(2,1)}), bf16[64,64,2,256]{3,1,2,0:T(8,128)(2,1)}) %all-gather.14.cloned.1.call-update) | async-done | bytes 4194320 | tf_op jit(solution)/shard_map/all_gather | solution.py:25
  352.5 38.0 %all-gather.16.cloned.1.call-done = bf16[128,64,2,256]{3,1,2,0:T(8,128)(2,1)} async-done(((bf16[64,64,2,256]{3,1,2,0:T(8,128)(2,1)}), bf16[128,64,2,256]{3,1,2,0:T(8,128)(2,1)}) %all-gather.16.cloned.1.call-update) | async-done | bytes 8388624 | tf_op jit(solution)/shard_map/all_gather | solution.py:25
  390.5 8.3 %copy.115 = bf16[16,4,2,64,2,256]{5,3,2,1,0,4:T(8,128)(2,1)} copy(bf16[16,4,2,64,2,256]{5,3,4,1,0,2:T(8,128)(2,1)} %bitcast.113) | data formatting | bytes 16777216 | tf_op jit(solution)/shard_map/transpose | solution.py:29
  398.7 5.7 %fusion.36 = (bf16[8192,1,256]{2,0,1:T(8,128)(2,1)}, bf16[8192,1,256]{2,0,1:T(8,128)(2,1)}) fusion(bf16[8192,2,256]{2,0,1:T(8,128)(2,1)} %bitcast.108), kind=kLoop, calls=%fused_computation.81 | loop fusion | bytes 16777216 | tf_op jit(solution)/shard_map/slice | solution.py:73
  404.4 6.4 %copy.116 = bf16[8192,1,256]{0,2,1:T(8,128)(2,1)} copy(bf16[8192,1,256]{2,0,1:T(8,128)(2,1)} %get-tuple-element.10) | data formatting | bytes 8388608 | tf_op jit(solution)/shard_map/slice | solution.py:74
  410.8 6.4 %copy.117 = bf16[8192,1,256]{0,2,1:T(8,128)(2,1)} copy(bf16[8192,1,256]{2,0,1:T(8,128)(2,1)} %get-tuple-element.9) | data formatting | bytes 8388608 | tf_op jit(solution)/shard_map/slice | solution.py:73
  417.2 3.1 fusion.40
  420.8 1.2 fusion.11
  (77 shorter events, 8.9 us)
Async XLA Ops:
  6.5 344.9 %copy-start = (s32[256,2]{0,1:T(2,128)S(1)}, s32[256,2]{0,1:T(2,128)}, u32[]{:S(2)}) copy-start(s32[256,2]{0,1:T(2,128)} %param.21) | copy-start | bytes 6148
  6.5 85.6 %copy-start.7 = (bf16[320,10]{0,1:T(8,128)(2,1)S(1)}, bf16[320,10]{0,1:T(8,128)(2,1)}, u32[]{:S(2)}) copy-start(bf16[320,10]{0,1:T(8,128)(2,1)} %param.14) | copy-start | bytes 19204
  6.5 81.7 %all-gather.8.cloned.1.call-start = ((), (), s32[]{:S(2)}) async-start(), calls=%async_computation.1 | async-start | bytes 2088960 | tf_op jit(solution)/shard_map/all_gather | solution.py:25
  19.1 186.1 %all-gather.10.cloned.1.call-start = ((), (), s32[]{:S(2)}) async-start(), calls=%async_computation.2 | async-start | bytes 4423680 | tf_op jit(solution)/shard_map/all_gather | solution.py:25
  91.3 113.6 %copy-start.10 = (s32[1,64]{1,0:T(1,128)S(1)}, s32[1,64]{1,0:T(1,128)}, u32[]{:S(2)}) copy-start(s32[1,64]{1,0:T(1,128)} %param.15) | copy-start | bytes 772
  91.3 113.6 %copy-start.2 = (bf16[256,1280]{1,0:T(8,128)(2,1)S(1)}, bf16[256,1280]{1,0:T(8,128)(2,1)}, u32[]{:S(2)}) copy-start(bf16[256,1280]{1,0:T(8,128)(2,1)} %param.11) | copy-start | bytes 1966084
  91.3 177.7 %all-gather.12.cloned.1.call-start = ((), (), s32[]{:S(2)}) async-start(), calls=%async_computation.3 | async-start | bytes 5283840 | tf_op jit(solution)/shard_map/all_gather | solution.py:141
  92.1 259.3 %all-gather.14.cloned.1.call-start = ((), (), s32[]{:S(2)}) async-start(), calls=%async_computation.4 | async-start | bytes 4456448 | tf_op jit(solution)/shard_map/all_gather | solution.py:25
  214.3 7.0 %copy-start.3 = (bf16[256,1280]{1,0:T(8,128)(2,1)S(1)}, bf16[256,1280]{1,0:T(8,128)(2,1)}, u32[]{:S(2)}) copy-start(bf16[256,1280]{1,0:T(8,128)(2,1)} %param.11) | copy-start | bytes 1966084
  214.3 7.0 %copy-start.9 = (f32[1280]{0:T(1024)S(1)}, f32[1280]{0:T(1024)}, u32[]{:S(2)}) copy-start(f32[1280]{0:T(1024)} %param.12) | copy-start | bytes 15364
  227.8 3.7 copy-start.4
  267.6 0.7 copy-start.8
  273.4 78.1 %copy-start.5 = (bf16[2,64,2,256]{3,2,1,0:T(2,128)(2,1)S(1)}, bf16[2,64,2,256]{3,2,1,0:T(2,128)(2,1)}, u32[]{:S(2)}) copy-start(bf16[2,64,2,256]{3,2,1,0:T(2,128)(2,1)} %param.19) | copy-start | bytes 393220
  273.5 78.5 %copy-start.11 = (s32[2]{0:T(128)S(1)}, s32[2]{0:T(128)}, u32[]{:S(2)}) copy-start(s32[2]{0:T(128)} %param.20) | copy-start | bytes 28
  273.5 78.6 %copy-start.6 = (bf16[2,2048]{1,0:T(2,128)(2,1)S(1)}, bf16[2,2048]{1,0:T(2,128)(2,1)}, u32[]{:S(2)}) copy-start(bf16[2,2048]{1,0:T(2,128)(2,1)} %param.18) | copy-start | bytes 24580
  284.6 105.8 %all-gather.16.cloned.1.call-start = ((), (), s32[]{:S(2)}) async-start(), calls=%async_computation.5 | async-start | bytes 12582912 | tf_op jit(solution)/shard_map/all_gather | solution.py:25
  417.2 3.6 copy-start.1
Sparse Core Ops, SparseCore 0:
  19.2 68.9 all-gather.7
  91.4 30.2 all-gather.9
  124.9 143.7 all-gather.11
  284.8 66.5 all-gather.13
  353.3 37.1 all-gather.15
where the time goes:
time: 430 us; the launch traced here: 429 us
  waiting for transfers between devices  175 us (41%)
  blocking collectives  170 us (40%)
  local copies, waits for them, and re-layouts  59.8 us (14%)
  between operations  13.5 us (3%)
  matrix products  9.15 us (2%)
    all_gather x4, waiting for transfers between devices, all_blocks(): blocks = lax.all_gather(blocks, axes[k], axis=0, tiled=True)  174 us
    all_gather x1, blocking collectives, on_device(): w_full = lax.all_gather(w_out, SEQ, axis=1, tiled=True)  111 us
    all_to_all x1, blocking collectives, from_everyone(): return lax.all_to_all(copies, axis, split_axis=0, concat_axis=0, tiled=True)  35.4 us
    all_gather x2, blocking collectives, all_blocks(): blocks = lax.all_gather(blocks, axes[k], axis=0, tiled=True)  23.6 us
    transpose x2, local copies, waits for them, and re-layouts, all_blocks(): blocks.transpose(*turned, *range(len(sequence), blocks.ndim))  12.7 us
    slice x2, local copies, waits for them, and re-layouts, prefix_scores(): keys = keys_values[:, 0].reshape(token_count, kv_local, head_size)  12.1 us
  transfers between devices with their start and end apart: 5, of which 3 were waited for; matrix products, arithmetic and copies ran while one was open for 7% of the time, Pallas kernels for 0%

commit v1 on v0

--- a/solution.py
+++ b/solution.py
@@ -1,3 +1,4 @@
+import functools
 import jax
 import jax.numpy as jnp
 from jax import lax
@@ -11,6 +12,16 @@
 WIN = 64
 SEQ = ("seq_0", "seq_1", "seq_2")
 NEGATIVE = -1e30
+
+
+def make_forms_now(view, chip_axis, array_dim):
+    return jnp.concatenate(
+        lax.all_to_all(jnp.stack([view] * lax.axis_size(chip_axis), axis=0), chip_axis, 0, 0),
+        axis=array_dim,
+    )
+
+
+keep_up_scenes = functools.partial(make_forms_now, chip_axis=SEQ, array_dim=1)
 
 
 def in_order(blocks, dim):
@@ -129,7 +140,7 @@
         lambda frame_rows, unit_order: frame_window(frame_rows, unit_order, local_heads, head_size)
     )(projected, window_order)
     attended = attended.reshape(row_count, columns)
-    w_full = lax.all_gather(w_out, SEQ, axis=1, tiled=True)
+    w_full = keep_up_scenes(w_out)
     summed = of_everyone(
         jnp.dot(attended, w_full, preferred_element_type=jnp.float32).astype(jnp.bfloat16), "head"
     ).astype(jnp.float32)

time: 430 us -> 437 us (1.016)
  blocking collectives: 170 us -> 55 us
  waiting for transfers between devices: 175 us -> 274 us
  starting transfers between devices: 0.17 us -> 22.1 us
    all_gather x1 -> x0, blocking collectives: 111 us -> none  [on_device(): w_full = lax.all_gather(w_out, SEQ, axis=1, tiled=True)]
    all_to_all x0 -> x1, waiting for transfers between devices: none -> 75.3 us  [make_forms_now(): lax.all_to_all(jnp.stack([view] * lax.axis_size(chip_axis), axis=0), chip...]
    all_gather x1, waiting for transfers between devices: 0.02 us -> 23 us  [on_device(): portion = lax.all_gather(w_kv, SEQ, axis=0, tiled=True)]
    all_to_all x0 -> x1, starting transfers between devices: none -> 21.7 us  [make_forms_now(): lax.all_to_all(jnp.stack([view] * lax.axis_size(chip_axis), axis=0), chip...]
  transfers between devices with their start and end apart: 5 -> 6, of which waited for: 3 -> 5; matrix products, arithmetic and copies ran while one was open for 7% -> 7% of each run, Pallas kernels for 0% -> 0%
where the time goes in v1:
time: 437 us; the launch traced here: 436 us
  waiting for transfers between devices  274 us (63%)
  local copies, waits for them, and re-layouts  60.8 us (14%)
  blocking collectives  55 us (13%)
  starting transfers between devices  22.1 us (5%)
  between operations  13.5 us (3%)
  matrix products  9.17 us (2%)
    all_gather x4, waiting for transfers between devices, all_blocks(): blocks = lax.all_gather(blocks, axes[k], axis=0, tiled=True)  175 us
    all_to_all x1, waiting for transfers between devices, make_forms_now(): lax.all_to_all(jnp.stack([view] * lax.axis_size(chip_axis), axis=0), chip...  75.3 us
    all_to_all x1, blocking collectives, from_everyone(): return lax.all_to_all(copies, axis, split_axis=0, concat_axis=0, tiled=True)  32.2 us
    all_gather x1, waiting for transfers between devices, on_device(): portion = lax.all_gather(w_kv, SEQ, axis=0, tiled=True)  23 us
    all_gather x2, blocking collectives, all_blocks(): blocks = lax.all_gather(blocks, axes[k], axis=0, tiled=True)  22.8 us
    all_to_all x1, starting transfers between devices, make_forms_now(): lax.all_to_all(jnp.stack([view] * lax.axis_size(chip_axis), axis=0), chip...  21.7 us
    transpose x2, local copies, waits for them, and re-layouts, all_blocks(): blocks.transpose(*turned, *range(len(sequence), blocks.ndim))  12.7 us
    slice x2, local copies, waits for them, and re-layouts, prefix_scores(): keys = keys_values[:, 0].reshape(token_count, kv_local, head_size)  12.1 us
  transfers between devices with their start and end apart: 6, of which 5 were waited for; matrix products, arithmetic and copies ran while one was open for 7% of the time, Pallas kernels for 0%

profile of v1, /device:TPU:1, one launch (start us, length us, event | category | flops | bytes accessed | tf_op | source)
XLA Modules:
  0.0 436.4 jit_solution(7356428745116236303)
XLA Ops:
  6.5 12.5 %all-gather = bf16[40,3,320]{2,1,0:T(4,128)(2,1)} all-gather(bf16[10,3,320]{2,1,0:T(4,128)(2,1)} %param.13), channel_id=2, replica_groups=mesh['seq_0'=16,'seq_1'=4,'seq_2'=2,'head'=4] {'seq_1'}, dimensions={0}, use_global_device_ids=true | all-gather | bytes 96000 | tf_op jit(solution)/shard_map/all_gather | solution.py:36
  19.1 69.1 %all-gather.7.cloned.1.call-done = bf16[64,10,3,320]{3,2,1,0:T(4,128)(2,1)} async-done(((bf16[4,10,3,320]{3,2,1,0:T(4,128)(2,1)}), bf16[64,10,3,320]{3,2,1,0:T(4,128)(2,1)}) %all-gather.7.cloned.1.call-update) | async-done | bytes 1228816 | tf_op jit(solution)/shard_map/all_gather | solution.py:36
  88.2 2.9 copy.105
  92.0 1.4 stack.2
  93.4 21.7 %all-to-all-start = ((bf16[128,320,10]{1,2,0:T(8,128)(2,1)}), bf16[128,320,10]{1,2,0:T(8,128)(2,1)S(1)}, u32[]{:S(2)}, u32[]{:S(2)}) async-start(bf16[128,320,10]{1,2,0:T(8,128)(2,1)} %stack.2), calls=%async_computation | async-start | bytes 3145728 | tf_op jit(solution)/shard_map/all_to_all | solution.py:19
  115.6 75.3 %all-to-all-done = bf16[128,320,10]{1,2,0:T(8,128)(2,1)S(1)} async-done(((bf16[128,320,10]{1,2,0:T(8,128)(2,1)}), bf16[128,320,10]{1,2,0:T(8,128)(2,1)S(1)}, u32[]{:S(2)}, u32[]{:S(2)}) %all-to-all-start) | async-done | bytes 819232 | tf_op jit(solution)/shard_map/all_to_all | solution.py:19
  190.9 1.4 reshape.195
  192.3 4.6 %reshape.187 = bf16[2,16,4,10,3,320]{5,2,1,0,4,3:T(4,128)(2,1)S(1)} reshape(bf16[128,10,3,320]{3,0,2,1:T(8,128)(2,1)} %all-gather.9.cloned.1.call-done) | data formatting | bytes 4915200 | tf_op jit(solution)/shard_map/reshape | solution.py:38
  197.0 4.5 %copy.106 = bf16[16,4,2,10,3,320]{5,4,3,2,1,0:T(4,128)(2,1)} copy(bf16[16,4,2,10,3,320]{5,1,0,2,4,3:T(4,128)(2,1)S(1)} %bitcast.112) | data formatting | bytes 4915200 | tf_op jit(solution)/shard_map/transpose | solution.py:40
  201.5 6.9 %reshape_reshape_reshape.3 = bf16[1280,960]{1,0:T(8,128)(2,1)S(1)} reshape(bf16[16,4,2,10,3,320]{5,4,3,2,1,0:T(4,128)(2,1)} %copy.106) | data formatting | bytes 4915200 | tf_op jit(solution)/shard_map/reshape;reshape;reshape | solution.py:136
  208.4 2.0 convolution_convert_fusion.1
  210.4 1.2 copy.107
  216.1 2.5 scatter_fusion
  219.3 32.2 %all_to_all.10 = bf16[4,256,1280]{2,1,0:T(8,128)(2,1)S(1)} all-to-all(bf16[4,256,1280]{2,1,0:T(8,128)(2,1)S(1)} %broadcast_in_dim.37), channel_id=1, replica_groups=mesh['seq_0'=16,'seq_1'=4,'seq_2'=2,'head'=4] {'head'}, dimensions={0} | all-to-all | bytes 5242880 | tf_op jit(solution)/shard_map/all_to_all | solution.py:49
  252.9 23.0 %all-gather.11.cloned.1.call-done = bf16[5120,2,256]{2,1,0:T(2,128)(2,1)} async-done(((bf16[40,2,256]{2,1,0:T(2,128)(2,1)}), bf16[5120,2,256]{2,1,0:T(2,128)(2,1)}) %all-gather.11.cloned.1.call-update) | async-done | bytes 5242896 | tf_op jit(solution)/shard_map/all_gather | solution.py:152
  275.9 3.4 copy.145
  280.4 10.2 %all_gather.25 = bf16[4,64,2,256]{3,1,2,0:T(8,128)(2,1)} all-gather(bf16[1,64,2,256]{3,1,2,0:T(8,128)(2,1)S(1)} %copy.115), channel_id=1, replica_groups=mesh['seq_0'=16,'seq_1'=4,'seq_2'=2,'head'=4] {'seq_1'}, dimensions={0}, use_global_device_ids=true | all-gather | bytes 327680 | tf_op jit(solution)/shard_map/all_gather | solution.py:36
  290.7 67.8 %all-gather.13.cloned.1.call-done = bf16[64,64,2,256]{3,1,2,0:T(8,128)(2,1)} async-done(((bf16[4,64,2,256]{3,1,2,0:T(8,128)(2,1)}), bf16[64,64,2,256]{3,1,2,0:T(8,128)(2,1)}) %all-gather.13.cloned.1.call-update) | async-done | bytes 4194320 | tf_op jit(solution)/shard_map/all_gather | solution.py:36
  359.6 38.0 %all-gather.15.cloned.1.call-done = bf16[128,64,2,256]{3,1,2,0:T(8,128)(2,1)} async-done(((bf16[64,64,2,256]{3,1,2,0:T(8,128)(2,1)}), bf16[128,64,2,256]{3,1,2,0:T(8,128)(2,1)}) %all-gather.15.cloned.1.call-update) | async-done | bytes 8388624 | tf_op jit(solution)/shard_map/all_gather | solution.py:36
  397.6 8.3 %copy.116 = bf16[16,4,2,64,2,256]{5,3,2,1,0,4:T(8,128)(2,1)} copy(bf16[16,4,2,64,2,256]{5,3,4,1,0,2:T(8,128)(2,1)} %bitcast.113) | data formatting | bytes 16777216 | tf_op jit(solution)/shard_map/transpose | solution.py:40
  405.8 5.7 %fusion.36 = (bf16[8192,1,256]{2,0,1:T(8,128)(2,1)}, bf16[8192,1,256]{2,0,1:T(8,128)(2,1)}) fusion(bf16[8192,2,256]{2,0,1:T(8,128)(2,1)} %bitcast.108), kind=kLoop, calls=%fused_computation.81 | loop fusion | bytes 16777216 | tf_op jit(solution)/shard_map/slice | solution.py:84
  411.5 6.3 %copy.117 = bf16[8192,1,256]{0,2,1:T(8,128)(2,1)} copy(bf16[8192,1,256]{2,0,1:T(8,128)(2,1)} %get-tuple-element.10) | data formatting | bytes 8388608 | tf_op jit(solution)/shard_map/slice | solution.py:85
  417.9 6.4 %copy.118 = bf16[8192,1,256]{0,2,1:T(8,128)(2,1)} copy(bf16[8192,1,256]{2,0,1:T(8,128)(2,1)} %get-tuple-element.9) | data formatting | bytes 8388608 | tf_op jit(solution)/shard_map/slice | solution.py:84
  424.2 3.1 fusion.40
  (79 shorter events, 12.4 us)
Async XLA Ops:
  6.5 352.0 %copy-start = (s32[256,2]{0,1:T(2,128)S(1)}, s32[256,2]{0,1:T(2,128)}, u32[]{:S(2)}) copy-start(s32[256,2]{0,1:T(2,128)} %param.21) | copy-start | bytes 6148
  6.5 85.4 %copy-start.7 = (bf16[320,10]{0,1:T(8,128)(2,1)S(1)}, bf16[320,10]{0,1:T(8,128)(2,1)}, u32[]{:S(2)}) copy-start(bf16[320,10]{0,1:T(8,128)(2,1)} %param.14) | copy-start | bytes 19204
  6.5 81.7 %all-gather.7.cloned.1.call-start = ((), (), s32[]{:S(2)}) async-start(), calls=%async_computation.2 | async-start | bytes 2088960 | tf_op jit(solution)/shard_map/all_gather | solution.py:36
  19.1 173.2 %all-gather.9.cloned.1.call-start = ((), (), s32[]{:S(2)}) async-start(), calls=%async_computation.3 | async-start | bytes 4423680 | tf_op jit(solution)/shard_map/all_gather | solution.py:36
  91.2 24.1 %copy-start.10 = (s32[1,64]{1,0:T(1,128)S(1)}, s32[1,64]{1,0:T(1,128)}, u32[]{:S(2)}) copy-start(s32[1,64]{1,0:T(1,128)} %param.15) | copy-start | bytes 772
  91.2 24.2 %copy-start.2 = (bf16[256,1280]{1,0:T(8,128)(2,1)S(1)}, bf16[256,1280]{1,0:T(8,128)(2,1)}, u32[]{:S(2)}) copy-start(bf16[256,1280]{1,0:T(8,128)(2,1)} %param.11) | copy-start | bytes 1966084
  91.2 184.7 %all-gather.11.cloned.1.call-start = ((), (), s32[]{:S(2)}) async-start(), calls=%async_computation.4 | async-start | bytes 5283840 | tf_op jit(solution)/shard_map/all_gather | solution.py:152
  93.4 97.6 %all-to-all-start = ((bf16[128,320,10]{1,2,0:T(8,128)(2,1)}), bf16[128,320,10]{1,2,0:T(8,128)(2,1)S(1)}, u32[]{:S(2)}, u32[]{:S(2)}) async-start(bf16[128,320,10]{1,2,0:T(8,128)(2,1)} %stack.2), calls=%async_computation | async-start | bytes 3145728 | tf_op jit(solution)/shard_map/all_to_all | solution.py:19
  115.1 243.4 %all-gather.13.cloned.1.call-start = ((), (), s32[]{:S(2)}) async-start(), calls=%async_computation.5 | async-start | bytes 4456448 | tf_op jit(solution)/shard_map/all_gather | solution.py:36
  201.4 6.9 %copy-start.3 = (bf16[256,1280]{1,0:T(8,128)(2,1)S(1)}, bf16[256,1280]{1,0:T(8,128)(2,1)}, u32[]{:S(2)}) copy-start(bf16[256,1280]{1,0:T(8,128)(2,1)} %param.11) | copy-start | bytes 1966084
  201.5 6.9 %copy-start.9 = (f32[1280]{0:T(1024)S(1)}, f32[1280]{0:T(1024)}, u32[]{:S(2)}) copy-start(f32[1280]{0:T(1024)} %param.12) | copy-start | bytes 15364
  214.9 3.7 copy-start.4
  251.5 0.7 copy-start.8
  280.3 78.3 %copy-start.5 = (bf16[2,64,2,256]{3,2,1,0:T(2,128)(2,1)S(1)}, bf16[2,64,2,256]{3,2,1,0:T(2,128)(2,1)}, u32[]{:S(2)}) copy-start(bf16[2,64,2,256]{3,2,1,0:T(2,128)(2,1)} %param.19) | copy-start | bytes 393220
  280.4 78.8 %copy-start.11 = (s32[2]{0:T(128)S(1)}, s32[2]{0:T(128)}, u32[]{:S(2)}) copy-start(s32[2]{0:T(128)} %param.20) | copy-start | bytes 28
  280.4 78.8 %copy-start.6 = (bf16[2,2048]{1,0:T(2,128)(2,1)S(1)}, bf16[2,2048]{1,0:T(2,128)(2,1)}, u32[]{:S(2)}) copy-start(bf16[2,2048]{1,0:T(2,128)(2,1)} %param.18) | copy-start | bytes 24580
  290.7 106.9 %all-gather.15.cloned.1.call-start = ((), (), s32[]{:S(2)}) async-start(), calls=%async_computation.6 | async-start | bytes 12582912 | tf_op jit(solution)/shard_map/all_gather | solution.py:36
  424.2 3.6 copy-start.1
Sparse Core Ops, SparseCore 0:
  19.2 68.9 all-gather.6
  91.3 30.2 all-gather.8
  124.8 151.1 all-gather.10
  290.8 67.6 all-gather.12
  360.4 37.1 all-gather.14
